TPU v7x, 32 devices: a whole 2x2x4 slice. The times are simulated.
32 devices in a mesh: gx: 16 (over z, x, core), gy: 2 (over y).
Axes of the slice: x: 2, y: 2, z: 4, core: 2. Of those that a mesh axis runs over, the one named last changes fastest.
Arguments:
- conc: float32 [32, 1024, 256], P(None, 'gx', 'gy'), may hold values from -4 to 4
- mobility: float32 [32, 1024, 256], P(None, 'gx', 'gy'), may hold values from 0.3 to 3
- block_x: float32 [32, 1024, 64], P(None, 'gx'), may hold values from -0.75 to 0.75
- spike_x: float32 [32, 1024, 4], P(None, 'gx'), may hold values from -3 to 3
- reduced_x: float32 [32, 64, 64], replicated, may hold values from -0.75 to 0.75
- block_y: float32 [32, 256, 128], P(None, 'gy'), may hold values from -0.5 to 0.5
- spike_y: float32 [32, 256, 4], P(None, 'gy'), may hold values from -3 to 3
- reduced_y: float32 [32, 8, 8], replicated, may hold values from -2 to 2
Outputs:
- conc_next: float32 [32, 1024, 256], P(None, 'gx', 'gy')
All inputs are finite; a program needn't handle non-finite values.
Results may differ from a plain program's by a relative error of at most 0.00012.
Values sent between devices are 32-bit elements; how exact they have to be, the bound alone decides.
A program may use at most 64 MiB of HBM per device.

v0:
```python
import jax
import jax.numpy as jnp
from jax import lax
from jax.sharding import PartitionSpec as P

HIGH = lax.Precision.HIGHEST


def extended_2(shard, sides, width):
    for axis, dim in sides:
        devices, length = (lax.axis_size(axis), shard.shape[dim])
        up = [(i, (i + 1) % devices) for i in range(devices)]
        down = [(j, i) for i, j in up]
        last = lax.slice_in_dim(shard, length - width, length, axis=dim)
        leading = lax.slice_in_dim(shard, 0, width, axis=dim)
        before = lax.ppermute(last, axis, up)
        after = lax.ppermute(leading, axis, down)
        shard = jnp.concatenate([before, shard, after], axis=dim)
    return shard


def divergence(conc, mu_ext, mob_ext):
    mu_mid = mu_ext[:, 1:-1, 1:-1]
    mob_mid = mob_ext[:, 1:-1, 1:-1]
    total = jnp.zeros_like(conc)
    for lo_x, hi_x, lo_y, hi_y in (
        (2, None, 1, -1),
        (0, -2, 1, -1),
        (1, -1, 2, None),
        (1, -1, 0, -2),
    ):
        mu_side = mu_ext[:, lo_x:hi_x, lo_y:hi_y]
        mob_side = mob_ext[:, lo_x:hi_x, lo_y:hi_y]
        total = total + 0.5 * (mob_side + mob_mid) * (mu_side - mu_mid)
    return conc + 0.02 * total


def laplace(padded):
    return (
        padded[:, 2:, 1:-1]
        + padded[:, :-2, 1:-1]
        + padded[:, 1:-1, 2:]
        + padded[:, 1:-1, :-2]
        - 4.0 * padded[:, 1:-1, 1:-1]
    )


def potential(centre, lap):
    return centre * centre * centre - centre - 1.0 * lap


def mobile(prefactor, centre):
    sq = centre * centre
    return prefactor * (0.25 + sq) / (1.0 + sq)


def solve_x(field, block_x, spike_x, reduced_x):
    width = field.shape[1]
    lin = jnp.einsum("zij,zjn->zin", block_x, field, precision=HIGH)
    rims = jnp.concatenate([lin[:, 0:2], lin[:, width - 2 :]], axis=1)
    whole = reduced_x.shape[1]
    place = lax.axis_index("gx")
    gathered = lax.all_gather(rims, "gx", axis=1, tiled=True)
    offsets = jnp.array([-2, -1, 4, 5], jnp.int32)
    picks = (4 * place + offsets) % whole
    rows_used = jnp.take(reduced_x, picks, axis=1)
    coupled = jnp.einsum("zrk,zkn->zrn", rows_used, gathered, precision=HIGH)
    return lin - jnp.einsum("zik,zkn->zin", spike_x, coupled, precision=HIGH)


def solve_y(field, block_y, spike_y, reduced_y):
    width = field.shape[2]
    lin = jnp.einsum("zij,zxj->zxi", block_y, field, precision=HIGH)
    rims = jnp.transpose(
        jnp.concatenate([lin[:, :, 0:2], lin[:, :, width - 2 :]], axis=2), (0, 2, 1)
    )
    gathered = lax.all_gather(rims, "gy", axis=1, tiled=True)
    whole = reduced_y.shape[1]
    place = lax.axis_index("gy")
    offsets = jnp.array([-2, -1, 4, 5], jnp.int32)
    picks = (4 * place + offsets) % whole
    rows_used = jnp.take(reduced_y, picks, axis=1)
    coupled = jnp.einsum("zrk,zkx->zrx", rows_used, gathered, precision=HIGH)
    return lin - jnp.einsum("zik,zkx->zxi", spike_y, coupled, precision=HIGH)


def body(conc, mobility, block_x, spike_x, reduced_x, block_y, spike_y, reduced_y):
    padded = extended_2(conc, (("gx", 1), ("gy", 2)), 1)
    mu_here = potential(conc, laplace(padded))
    mob_here = mobile(mobility, conc)
    extended = extended_2(jnp.stack([mu_here, mob_here]), (("gx", 2), ("gy", 3)), 1)
    rhs = divergence(conc, extended[0], extended[1])
    xsol = solve_x(rhs, block_x, spike_x, reduced_x)
    return solve_y(xsol, block_y, spike_y, reduced_y)


def solution(mesh):
    in_specs = (
        P(None, "gx", "gy"),
        P(None, "gx", "gy"),
        P(None, "gx", None),
        P(None, "gx", None),
        P(),
        P(None, "gy", None),
        P(None, "gy", None),
        P(),
    )
    out_specs = P(None, "gx", "gy")
    return jax.shard_map(body, mesh=mesh, in_specs=in_specs, out_specs=out_specs, check_vma=False)
```

profile of v0, /device:TPU:0, one launch (start us, length us, event | category | flops | bytes accessed | tf_op | source)
XLA Modules:
  0.0 137.7 jit_solution(11879824892169234016)
XLA Ops:
  7.7 5.5 %collective-permute-start = (f32[32,1,128]{2,0,1:T(8,128)S(1)}, f32[32,1,128]{2,0,1:T(8,128)S(1)}, u32[]{:S(2)}, u32[]{:S(2)}) collective-permute-start(f32[32,1,128]{2,0,1:T(8,128)S(1)} %bitcast.50), channel_id=1, source_target_pairs={{2,0},{4,2},{6,4},{8,6},{10,8},{12,10},{14,12},{16,14},{18,16},{20... | collective-permute-start | bytes 49160 | tf_op jit(solution)/shard_map/ppermute | solution.py:17
  14.6 4.4 %collective-permute-done.1 = f32[32,1,128]{2,0,1:T(8,128)S(1)} collective-permute-done((f32[32,1,128]{2,0,1:T(8,128)S(1)}, f32[32,1,128]{2,0,1:T(8,128)S(1)}, u32[]{:S(2)}, u32[]{:S(2)}) %collective-permute-start.1) | collective-permute-done | bytes 16416 | tf_op jit(solution)/shard_map/ppermute | solution.py:16
  21.8 1.7 %copy.63 = f32[32,66,1]{1,0,2:T(8,128)S(1)} copy(f32[32,66,1]{2,1,0:T(8,128)} %get-tuple-element.15) | data formatting | bytes 16896 | tf_op jit(solution)/shard_map/slice | solution.py:15
  23.5 1.6 %collective-permute-start.2 = (f32[32,66,1]{1,0,2:T(8,128)S(1)}, f32[32,66,1]{1,0,2:T(8,128)S(1)}, u32[]{:S(2)}, u32[]{:S(2)}) collective-permute-start(f32[32,66,1]{1,0,2:T(8,128)S(1)} %copy.63), channel_id=1, source_target_pairs={{1,0},{0,1},{3,2},{2,3},{5,4},{4,5},{7,6},{6,7},{9,8},{8,9},{11,10... | collective-permute-start | bytes 25352 | tf_op jit(solution)/shard_map/ppermute | solution.py:17
  30.8 5.3 %fusion.5 = (f32[1,32,64,128]{3,2,1,0:T(8,128)S(1)}, f32[1,32,64,128]{3,2,1,0:T(8,128)S(1)}) fusion(f32[32,64,128]{2,1,0:T(8,128)} %param.10, f32[32,66,1]{2,1,0:T(8,128)} %copy.66, f32[32,1,128]{2,1,0:T(1,128)S(1)} %bitcast.44, f32[32,1,128]{2,1,0:T(1,128)S(1)} %bitcast.46, f32[32,66,1]{2,1,0:T(8,128)} %copy.64, f32[32,64,128]{2,1,0:T(8,128)} %param.11), kind=kLoop, calls=%fused_computation.18 | loop fusion | flops 5505024 | bytes 4243968 | tf_op jit(solution)/shard_map/stack | solution.py:91
  36.2 4.4 %collective-permute-start.5 = (f32[2,32,1,128]{3,1,2,0:T(8,128)S(1)}, f32[2,32,1,128]{3,1,2,0:T(8,128)S(1)}, u32[]{:S(2)}, u32[]{:S(2)}) collective-permute-start(f32[2,32,1,128]{3,1,2,0:T(8,128)S(1)} %bitcast.47), channel_id=1, source_target_pairs={{2,0},{4,2},{6,4},{8,6},{10,8},{12,10},{14,12},{16,14},{18,16},{20... | collective-permute-start | bytes 98312 | tf_op jit(solution)/shard_map/ppermute | solution.py:17
  40.7 1.6 %collective-permute-done.4 = f32[2,32,1,128]{3,1,2,0:T(8,128)S(1)} collective-permute-done((f32[2,32,1,128]{3,1,2,0:T(8,128)S(1)}, f32[2,32,1,128]{3,1,2,0:T(8,128)S(1)}, u32[]{:S(2)}, u32[]{:S(2)}) %collective-permute-start.4) | collective-permute-done | bytes 32800 | tf_op jit(solution)/shard_map/ppermute | solution.py:16
  42.6 2.9 %fusion.48 = (f32[2,32,66,1]{3,2,1,0:T(8,128)}, f32[2,32,66,1]{3,2,1,0:T(8,128)}) fusion(f32[2,32,66,128]{3,2,1,0:T(8,128)S(1)} %pad_maximum_fusion.1), kind=kLoop, calls=%fused_computation.86 | loop fusion | bytes 67584 | tf_op jit(solution)/shard_map/slice | solution.py:14
  45.5 2.4 %copy.71 = f32[2,32,66,1]{2,1,3,0:T(8,128)S(1)} copy(f32[2,32,66,1]{3,2,1,0:T(8,128)} %get-tuple-element.11) | data formatting | bytes 33792 | tf_op jit(solution)/shard_map/slice | solution.py:14
  49.0 2.4 %copy.72 = f32[2,32,66,1]{2,1,3,0:T(8,128)S(1)} copy(f32[2,32,66,1]{3,2,1,0:T(8,128)} %get-tuple-element.12) | data formatting | bytes 33792 | tf_op jit(solution)/shard_map/slice | solution.py:15
  52.5 2.3 %copy.73 = f32[2,32,66,1]{3,2,1,0:T(8,128)} copy(f32[2,32,66,1]{2,1,3,0:T(8,128)S(1)} %collective-permute-done.6) | data formatting | bytes 33792 | tf_op jit(solution)/shard_map/ppermute | solution.py:16
  55.4 2.3 %copy.74 = f32[2,32,66,1]{3,2,1,0:T(8,128)} copy(f32[2,32,66,1]{2,1,3,0:T(8,128)S(1)} %collective-permute-done.7) | data formatting | bytes 33792 | tf_op jit(solution)/shard_map/ppermute | solution.py:17
  57.7 5.4 %pad_maximum_fusion = f32[2,32,66,130]{3,2,1,0:T(8,128)S(1)} fusion(f32[2,32,66,1]{3,2,1,0:T(8,128)} %copy.74, f32[2,32,1,128]{3,2,1,0:T(1,128)S(1)} %bitcast.42, f32[1,32,64,128]{3,2,1,0:T(8,128)} %copy-done.1, f32[1,32,64,128]{3,2,1,0:T(8,128)S(1)} %get-tuple-element.21, f32[2,32,1,128]{3,2,1,0:T(1,128)S(1)} %bitcast.40, f32[2,32,66,1]{3,2,1,0:T(8,128)} %copy.73), kind=kLoop, calls=%fused_computation.2 | loop fusion | flops 2745600 | bytes 4392960 | tf_op jit(solution)/shard_map/concatenate | solution.py:18
  64.3 5.3 %convolution_bitcast_fusion.1 = f32[32,64,128]{2,1,0:T(8,128)} fusion(f32[32,64,64]{2,1,0:T(8,128)} %param.12, f32[32,64,128]{2,1,0:T(8,128)S(1)} %copy-done.2, f32[32,66,130]{2,1,0:T(8,128)S(1)} %get-tuple-element.10, f32[32,66,130]{2,1,0:T(8,128)S(1)} %get-tuple-element.9), kind=kOutput, calls=%fused_computation.12 | convolution fusion | flops 206831616 | bytes 13107200 | tf_op jit(solution)/shard_map/zij,zjn->zin/dot_general | solution.py:59
  72.3 1.6 %gather_fusion = f32[4,32,64]{2,0,1:T(4,128)S(1)} fusion(f32[32,64,64]{2,1,0:T(8,128)} %param.14, s32[1024]{0:T(1024)S(1)} %pad_clamp_fusion.1), kind=kCustom, calls=%fused_computation | custom fusion | bytes 65552 | tf_op jit(solution)/shard_map/jit(_take)/gather | solution.py:66
  73.8 35.2 %all-gather.2.cloned.1.call-done = f32[32,64,128]{2,0,1:T(8,128)} async-done(((f32[32,4,128]{2,0,1:T(8,128)}), f32[32,64,128]{2,0,1:T(8,128)}) %all-gather.2.cloned.1.call-update) | async-done | bytes 1048592 | tf_op jit(solution)/shard_map/all_gather | solution.py:63
  109.1 2.7 %fusion.33 = f32[32,4,128]{2,1,0:T(4,128)S(1)} fusion(f32[32,64,128]{2,0,1:T(8,128)} %all-gather.2.cloned.1.call-done, f32[4,32,64]{2,0,1:T(4,128)S(1)} %gather_fusion, pred[4]{0:T(512)(128)(4,1)S(1)} %get-tuple-element.25), kind=kOutput, calls=%fused_computation.54 | convolution fusion | flops 12591104 | bytes 1146884 | tf_op jit(solution)/shard_map/zrk,zkn->zrn/dot_general | solution.py:67
  111.7 1.8 %fusion = f32[32,64,128]{2,1,0:T(8,128)S(1)} fusion(f32[32,64,128]{2,1,0:T(8,128)S(1)} %copy-done.3, f32[32,4,128]{2,1,0:T(4,128)S(1)} %fusion.33, f32[32,64,4]{1,2,0:T(4,128)S(1)} %copy-done.5), kind=kOutput, calls=%fused_computation.11 | convolution fusion | flops 12845056 | bytes 2195456 | tf_op jit(solution)/shard_map/zik,zkn->zin/dot_general | solution.py:68
  113.6 4.1 %fusion.53 = f32[32,64,128]{2,1,0:T(8,128)S(1)} fusion(f32[32,64,128]{2,1,0:T(8,128)S(1)} %fusion, f32[32,128,128]{2,1,0:T(8,128)S(1)} %copy-done), kind=kOutput, calls=%fused_computation.91 | convolution fusion | flops 402653184 | bytes 4194304 | tf_op jit(solution)/shard_map/zij,zxj->zxi/dot_general | solution.py:73
  117.7 1.7 %fusion.50 = (f32[32,64,2]{2,1,0:T(8,128)}, f32[32,64,2]{2,1,0:T(8,128)}) fusion(f32[32,64,128]{2,1,0:T(8,128)S(1)} %fusion.53), kind=kLoop, calls=%fused_computation.88 | loop fusion | bytes 65536 | tf_op jit(solution)/shard_map/slice | solution.py:75
  119.4 1.6 %copy.77 = f32[32,64,2]{1,0,2:T(8,128)S(1)} copy(f32[32,64,2]{2,1,0:T(8,128)} %get-tuple-element.17) | data formatting | bytes 32768 | tf_op jit(solution)/shard_map/slice | solution.py:75
  121.1 1.6 %copy.78 = f32[32,64,2]{1,0,2:T(8,128)S(1)} copy(f32[32,64,2]{2,1,0:T(8,128)} %get-tuple-element.18) | data formatting | bytes 32768 | tf_op jit(solution)/shard_map/slice | solution.py:75
  122.7 4.9 %all_gather.7 = f32[32,8,64]{2,0,1:T(8,128)S(1)} all-gather(f32[32,4,64]{2,0,1:T(8,128)S(1)} %maximum_bitcast_fusion), channel_id=1, replica_groups=mesh['gx'=16,'gy'=2] {'gy'}, dimensions={1}, use_global_device_ids=true | all-gather | bytes 98304 | tf_op jit(solution)/shard_map/all_gather | solution.py:77
  128.1 2.8 %convolution_subtract_fusion = f32[32,64,128]{2,1,0:T(8,128)} fusion(f32[32,64,128]{2,1,0:T(8,128)S(1)} %fusion.53, f32[32,4,64]{2,1,0:T(4,128)S(1)} %fusion.37, f32[32,128,4]{1,2,0:T(4,128)S(1)} %copy-done.6), kind=kOutput, calls=%fused_computation.9 | convolution fusion | flops 12845056 | bytes 2195456 | tf_op jit(solution)/shard_map/zik,zkx->zxi/dot_general | solution.py:84
  (49 shorter events, 18.5 us)
Async XLA Ops:
  6.5 107.0 %copy-start = (f32[32,128,128]{2,1,0:T(8,128)S(1)}, f32[32,128,128]{2,1,0:T(8,128)}, u32[]{:S(2)}) copy-start(f32[32,128,128]{2,1,0:T(8,128)} %param.15) | copy-start | bytes 6291460
  6.5 102.5 %all-gather.2.cloned.1.call-start = ((), (), s32[]{:S(2)}) async-start(), calls=%async_computation | async-start | bytes 1114112 | tf_op jit(solution)/shard_map/all_gather | solution.py:63
  7.7 6.9 %collective-permute-start = (f32[32,1,128]{2,0,1:T(8,128)S(1)}, f32[32,1,128]{2,0,1:T(8,128)S(1)}, u32[]{:S(2)}, u32[]{:S(2)}) collective-permute-start(f32[32,1,128]{2,0,1:T(8,128)S(1)} %bitcast.50), channel_id=1, source_target_pairs={{2,0},{4,2},{6,4},{8,6},{10,8},{12,10},{14,12},{16,14},{18,16},{20... | collective-permute-start | bytes 49160 | tf_op jit(solution)/shard_map/ppermute | solution.py:17
  13.2 5.9 %collective-permute-start.1 = (f32[32,1,128]{2,0,1:T(8,128)S(1)}, f32[32,1,128]{2,0,1:T(8,128)S(1)}, u32[]{:S(2)}, u32[]{:S(2)}) collective-permute-start(f32[32,1,128]{2,0,1:T(8,128)S(1)} %bitcast.49), channel_id=1, source_target_pairs={{0,2},{2,4},{4,6},{6,8},{8,10},{10,12},{12,14},{14,16},{16,18},{18... | collective-permute-start | bytes 49160 | tf_op jit(solution)/shard_map/ppermute | solution.py:16
  23.5 3.8 %collective-permute-start.2 = (f32[32,66,1]{1,0,2:T(8,128)S(1)}, f32[32,66,1]{1,0,2:T(8,128)S(1)}, u32[]{:S(2)}, u32[]{:S(2)}) collective-permute-start(f32[32,66,1]{1,0,2:T(8,128)S(1)} %copy.63), channel_id=1, source_target_pairs={{1,0},{0,1},{3,2},{2,3},{5,4},{4,5},{7,6},{6,7},{9,8},{8,9},{11,10... | collective-permute-start | bytes 25352 | tf_op jit(solution)/shard_map/ppermute | solution.py:17
  25.5 3.8 %collective-permute-start.3 = (f32[32,66,1]{1,0,2:T(8,128)S(1)}, f32[32,66,1]{1,0,2:T(8,128)S(1)}, u32[]{:S(2)}, u32[]{:S(2)}) collective-permute-start(f32[32,66,1]{1,0,2:T(8,128)S(1)} %copy.65), channel_id=1, source_target_pairs={{0,1},{1,0},{2,3},{3,2},{4,5},{5,4},{6,7},{7,6},{8,9},{9,8},{10,11... | collective-permute-start | bytes 25352 | tf_op jit(solution)/shard_map/ppermute | solution.py:16
  36.1 6.5 %copy-start.1 = (f32[1,32,64,128]{3,2,1,0:T(8,128)}, f32[1,32,64,128]{3,2,1,0:T(8,128)S(1)}, u32[]{:S(2)}) copy-start(f32[1,32,64,128]{3,2,1,0:T(8,128)S(1)} %get-tuple-element.22) | copy-start | bytes 3145732
  36.2 6.1 %collective-permute-start.4 = (f32[2,32,1,128]{3,1,2,0:T(8,128)S(1)}, f32[2,32,1,128]{3,1,2,0:T(8,128)S(1)}, u32[]{:S(2)}, u32[]{:S(2)}) collective-permute-start(f32[2,32,1,128]{3,1,2,0:T(8,128)S(1)} %bitcast.48), channel_id=1, source_target_pairs={{0,2},{2,4},{4,6},{6,8},{8,10},{10,12},{12,14},{14,16},{16,18},{18... | collective-permute-start | bytes 98312 | tf_op jit(solution)/shard_map/ppermute | solution.py:16
  36.2 6.0 %collective-permute-start.5 = (f32[2,32,1,128]{3,1,2,0:T(8,128)S(1)}, f32[2,32,1,128]{3,1,2,0:T(8,128)S(1)}, u32[]{:S(2)}, u32[]{:S(2)}) collective-permute-start(f32[2,32,1,128]{3,1,2,0:T(8,128)S(1)} %bitcast.47), channel_id=1, source_target_pairs={{2,0},{4,2},{6,4},{8,6},{10,8},{12,10},{14,12},{16,14},{18,16},{20... | collective-permute-start | bytes 98312 | tf_op jit(solution)/shard_map/ppermute | solution.py:17
  47.9 4.6 %collective-permute-start.6 = (f32[2,32,66,1]{2,1,3,0:T(8,128)S(1)}, f32[2,32,66,1]{2,1,3,0:T(8,128)S(1)}, u32[]{:S(2)}, u32[]{:S(2)}) collective-permute-start(f32[2,32,66,1]{2,1,3,0:T(8,128)S(1)} %copy.71), channel_id=1, source_target_pairs={{0,1},{1,0},{2,3},{3,2},{4,5},{5,4},{6,7},{7,6},{8,9},{9,8},{10,11... | collective-permute-start | bytes 50696 | tf_op jit(solution)/shard_map/ppermute | solution.py:16
  51.5 4.0 %collective-permute-start.7 = (f32[2,32,66,1]{2,1,3,0:T(8,128)S(1)}, f32[2,32,66,1]{2,1,3,0:T(8,128)S(1)}, u32[]{:S(2)}, u32[]{:S(2)}) collective-permute-start(f32[2,32,66,1]{2,1,3,0:T(8,128)S(1)} %copy.72), channel_id=1, source_target_pairs={{1,0},{0,1},{3,2},{2,3},{5,4},{4,5},{7,6},{6,7},{9,8},{8,9},{11,10... | collective-permute-start | bytes 50696 | tf_op jit(solution)/shard_map/ppermute | solution.py:17
  63.1 1.2 copy-start.2
  64.3 7.1 %copy-start.7 = (s32[4]{0:T(128)S(1)}, s32[4]{0:T(128)}, u32[]{:S(2)}) copy-start(s32[4]{0:T(128)} %constant.73.clone) | copy-start | bytes 52
  64.3 7.2 %copy-start.4 = (f32[32,8,8]{0,2,1:T(8,128)S(1)}, f32[32,8,8]{0,2,1:T(8,128)}, u32[]{:S(2)}) copy-start(f32[32,8,8]{0,2,1:T(8,128)} %param.17) | copy-start | bytes 24580
  69.7 42.1 %copy-start.3 = (f32[32,64,128]{2,1,0:T(8,128)S(1)}, f32[32,64,128]{2,1,0:T(8,128)}, u32[]{:S(2)}) copy-start(f32[32,64,128]{2,1,0:T(8,128)} %convolution_bitcast_fusion.1) | copy-start | bytes 3145732
  69.7 42.1 %copy-start.5 = (f32[32,64,4]{1,2,0:T(4,128)S(1)}, f32[32,64,4]{1,2,0:T(4,128)}, u32[]{:S(2)}) copy-start(f32[32,64,4]{1,2,0:T(4,128)} %param.13) | copy-start | bytes 98308
  119.4 8.6 %copy-start.6 = (f32[32,128,4]{1,2,0:T(4,128)S(1)}, f32[32,128,4]{1,2,0:T(4,128)}, u32[]{:S(2)}) copy-start(f32[32,128,4]{1,2,0:T(4,128)} %param.16) | copy-start | bytes 196612
Sparse Core Ops, SparseCore 0:
  71.6 37.4 all-gather.1
where the time goes:
time: 138 us
  waiting for transfers between devices  45.1 us (33%)
  local copies, waits for them, and re-layouts  30.1 us (22%)
  matrix products  17.2 us (12%)
  starting transfers between devices  14.2 us (10%)
  between operations  13.6 us (10%)
  other arithmetic  12.6 us (9%)
  blocking collectives  4.94 us (4%)
    all_gather x1, waiting for transfers between devices, solve_x(): gathered = lax.all_gather(rims, 'gx', axis=1, tiled=True)  35.2 us
    ppermute x4, starting transfers between devices, extended_2(): after = lax.ppermute(leading, axis, down)  12.5 us
    concatenate x3, other arithmetic, extended_2(): shard = jnp.concatenate([before, shard, after], axis=dim)  7.06 us
    slice x4, local copies, waits for them, and re-layouts, extended_2(): last = lax.slice_in_dim(shard, length - width, length, axis=dim)  6.89 us
    ppermute x4, waiting for transfers between devices, extended_2(): before = lax.ppermute(last, axis, up)  6.5 us
    slice x3, local copies, waits for them, and re-layouts, extended_2(): leading = lax.slice_in_dim(shard, 0, width, axis=dim)  5.55 us
    dot_general x1, matrix products, solve_x(): lin = jnp.einsum('zij,zjn->zin', block_x, field, precision=HIGH)  5.33 us
    another operation x1, other arithmetic, body(): jnp.stack([mu_here, mob_here])  5.33 us
  transfers between devices with their start and end apart: 9, of which 7 were waited for; matrix products, arithmetic and copies ran while one was open for 7% of the time, Pallas kernels for 0%

commit v1 on v0

v1 whole, which is shorter than its diff:
```python
import functools
import jax
import jax.numpy as jnp
from jax import lax
from jax.experimental import pallas as pl
from jax.experimental.pallas import tpu as pltpu
from jax.sharding import PartitionSpec as P

F32 = jnp.float32
BF16 = jnp.bfloat16
MESH = pl.DeviceIdType.MESH
HIGH = lax.Precision.HIGHEST


def split(value):
    hi = value.astype(BF16)
    lo = (value - hi.astype(F32)).astype(BF16)
    return hi, lo


def iota(shape, axis):
    return lax.broadcasted_iota(jnp.int32, shape, axis)


def mobile(prefactor, centre):
    sq = centre * centre
    return prefactor * (0.25 + sq) / (1.0 + sq)


def picks(place, j, whole):
    pick = 4 * place + jnp.where(j < 2, j - 2, j + 2)
    pick = jnp.where(pick < 0, pick + whole, pick)
    return jnp.where(pick >= whole, pick - whole, pick)


def kernel(
    n, m,
    conc_h, mob_h, bx_h, sx_h, rx_h, by_h, sy_h, ry_h, out_h,
    c_ref, b_ref, bx, sx, rx, by, sy, ry, out,
    xs_dn, xs_up, xr_dn, xr_up, ys, yr, cr,
    mux, mobx, mus, mobs, cs,
    bxc, byc, xl, yfull, rims, rrecv, recm, wsend, wrecv, sxp, yrims, ryc,
    load_sem, out_sem, xsem_s, xsem_r, ysem_s, ysem_r, csem_s, csem_r,
    a_s, a_r, w_s, w_r, g_s, g_r,
):
    NZ, X, Y = c_ref.shape
    owned = NZ // n
    R = 4 * n
    shift_owned = (4 * owned).bit_length() - 1
    i = lax.axis_index("gx")
    j = lax.axis_index("gy")
    up, dn = lax.rem(i + 1, n), lax.rem(i + n - 1, n)
    hi, lo = lax.rem(j + 1, m), lax.rem(j + m - 1, m)
    sides = (hi,) if m == 2 else (lo, hi)

    loads = [
        pltpu.make_async_copy(src, dst, load_sem.at[k])
        for k, (src, dst) in enumerate((
            (conc_h, c_ref), (mob_h, b_ref), (bx_h, bx), (sx_h, sx),
            (rx_h.at[pl.ds(i * owned, owned)], rx), (by_h, by), (sy_h, sy), (ry_h, ry),
        ))
    ]
    for load in loads:
        load.start()

    barrier = pltpu.get_barrier_semaphore()
    peers = [(lax.rem(i + t, n), j) for t in range(1, n)]
    peers += [(i, lax.rem(j + t, m)) for t in range(1, m)]
    peers += [(a, b) for a in (dn, up) for b in sides]
    for peer in peers:
        pl.semaphore_signal(barrier, inc=1, device_id=peer, device_id_type=MESH)

    loads[0].wait()
    loads[1].wait()
    xs_dn[0] = c_ref[:, 0, :]
    xs_dn[1] = c_ref[:, 1, :]
    xs_dn[2] = b_ref[:, 0, :]
    xs_up[0] = c_ref[:, X - 2, :]
    xs_up[1] = c_ref[:, X - 1, :]
    xs_up[2] = b_ref[:, X - 1, :]
    lane = iota((X, Y), 1)
    row = iota((X, Y), 0)
    group = lane >> 2
    pc = jnp.zeros((X, Y), F32)
    pb = jnp.zeros((X, Y), F32)
    for z in range(NZ):
        mine = group == z
        pc = jnp.where(mine, pltpu.roll(c_ref[z], (4 * z + 2) % Y, 1), pc)
        pb = jnp.where(mine, pltpu.roll(b_ref[z], (4 * z + 2) % Y, 1), pb)
    ys[0] = pc
    ys[1] = pb

    pl.semaphore_wait(barrier, len(peers))

    def remote(src, dst, ssem, rsem, who):
        return pltpu.make_async_remote_copy(
            src_ref=src, dst_ref=dst, send_sem=ssem, recv_sem=rsem,
            device_id=who, device_id_type=MESH)

    halo = [
        remote(xs_dn, xr_up, xsem_s.at[0], xsem_r.at[0], (dn, j)),
        remote(xs_up, xr_dn, xsem_s.at[1], xsem_r.at[1], (up, j)),
    ]
    for k, side in enumerate(sides):
        slot = k if m == 2 else 1 - k
        halo.append(remote(ys, yr.at[slot], ysem_s.at[k], ysem_r.at[k], (i, side)))
        halo.append(remote(ys.at[0, 0:8], cr.at[1, slot], csem_s.at[0, k], csem_r.at[0, k], (dn, side)))
        halo.append(remote(ys.at[0, X - 8:X], cr.at[0, slot], csem_s.at[1, k], csem_r.at[1, k], (up, side)))
    for copy in halo:
        copy.start()

    loads[2].wait()

    def prep_x(z, carry):
        h, l = split(bx[z])
        h32 = h.astype(F32)
        bxc[z, :, 0:2 * X] = jnp.concatenate([h32, h32], axis=1).astype(BF16)
        bxc[z, :, 2 * X:3 * X] = l
        return carry

    lax.fori_loop(0, NZ, prep_x, 0, unroll=4)

    for copy in halo:
        copy.wait_recv()

    lo_slot, hi_slot = (0, 0) if m == 2 else (0, 1)
    k4 = lane & 3
    low = k4 < 2
    pc = ys[0]
    ec = jnp.where(low, yr[lo_slot, 0], yr[hi_slot, 0])
    eb = jnp.where(low, yr[lo_slot, 1], yr[hi_slot, 1])
    low1 = low[0:1]
    cd = jnp.where(low1, cr[0, lo_slot, 7:8, :], cr[0, hi_slot, 7:8, :])
    cu = jnp.where(low1, cr[1, lo_slot, 0:1, :], cr[1, hi_slot, 0:1, :])
    fwd = lambda a: pltpu.roll(a, 1, 1)
    bwd = lambda a: pltpu.roll(a, Y - 1, 1)
    sum_y = jnp.where(low, fwd(ec) + bwd(pc), bwd(ec) + fwd(pc))
    sum_x = (jnp.where(row == 0, cd, pltpu.roll(ec, 1, 0))
             + jnp.where(row == X - 1, cu, pltpu.roll(ec, X - 1, 0)))
    emu = ec * ec * ec - ec - (sum_x + sum_y - 4.0 * ec)
    emob = mobile(eb, ec)
    swap = lambda a: jnp.where(k4 == 1, bwd(a), fwd(a))
    cs[...] = swap(ec)
    mus[...] = swap(emu)
    mobs[...] = swap(emob)

    zlane = iota((NZ, Y), 1)
    zrow = iota((NZ, Y), 0)
    for s, (near, far, own, corner) in enumerate((
        (xr_dn[1], xr_dn[0], xs_dn[0], cd),
        (xr_up[0], xr_up[1], xs_up[1], cu),
    )):
        c_lo = jnp.sum(jnp.where(zlane == 4 * zrow + 1, corner, 0.0), axis=1, keepdims=True)
        c_hi = jnp.sum(jnp.where(zlane == 4 * zrow + 2, corner, 0.0), axis=1, keepdims=True)
        side_lo = jnp.where(zlane == 0, c_lo, fwd(near))
        side_hi = jnp.where(zlane == Y - 1, c_hi, bwd(near))
        mux[s] = near * near * near - near - (far + own + side_lo + side_hi - 4.0 * near)
        mobx[s] = mobile((xr_dn if s == 0 else xr_up)[2], near)

    def plane_x(q, zz):
        z = q * owned + zz
        c = c_ref[z]
        unpack = Y - 2 - 4 * z
        cy = pltpu.roll(cs[...], unpack, 1)
        c_ym = jnp.where(lane == 0, cy, fwd(c))
        c_yp = jnp.where(lane == Y - 1, cy, bwd(c))
        c_xm = jnp.where(row == 0, xr_dn[1, pl.ds(z, 1), :], pltpu.roll(c, 1, 0))
        c_xp = jnp.where(row == X - 1, xr_up[0, pl.ds(z, 1), :], pltpu.roll(c, X - 1, 0))
        mu = c * c * c - c - (c_xm + c_xp + c_ym + c_yp - 4.0 * c)
        mob = mobile(b_ref[z], c)
        muy = pltpu.roll(mus[...], unpack, 1)
        moby = pltpu.roll(mobs[...], unpack, 1)
        fy = (jnp.where(lane == Y - 1, moby, bwd(mob)) + mob) * (jnp.where(lane == Y - 1, muy, bwd(mu)) - mu)
        fy_m = jnp.where(lane == 0, (mob + moby) * (mu - muy), fwd(fy))
        mu_dn, mu_up = mux[0, pl.ds(z, 1), :], mux[1, pl.ds(z, 1), :]
        mob_dn, mob_up = mobx[0, pl.ds(z, 1), :], mobx[1, pl.ds(z, 1), :]
        fx = ((jnp.where(row == X - 1, mob_up, pltpu.roll(mob, X - 1, 0)) + mob)
              * (jnp.where(row == X - 1, mu_up, pltpu.roll(mu, X - 1, 0)) - mu))
        fx_m = jnp.where(row == 0, (mob + mob_dn) * (mu - mu_dn), pltpu.roll(fx, 1, 0))
        rhs = c + 0.01 * ((fy - fy_m) + (fx - fx_m))
        rh, rl = split(rhs)
        lin = jnp.dot(bxc[z], jnp.concatenate([rh, rl, rh], axis=0), preferred_element_type=F32)
        xl[z] = lin
        rims[q, 4 * zz:4 * zz + 2, :] = lin[0:2]
        rims[q, 4 * zz + 2:4 * zz + 4, :] = lin[X - 2:X]

    def rim_copy(t):
        who = lax.rem(i + 1 + t, n)
        return remote(rims.at[who], rrecv.at[i], a_s.at[t], a_r.at[t], (who, j))

    def step_x(t, carry):
        who = lax.rem(i + 1 + t, n)
        for zz in range(owned):
            plane_x(who, zz)
        rim_copy(t).start()
        return carry

    lax.fori_loop(0, n - 1, step_x, 0)
    for zz in range(owned):
        plane_x(i, zz)
    rrecv[i] = rims[i]

    loads[4].wait()
    M = NZ * 4
    def parts_of(index):
        return index >> shift_owned, (index >> 2) & (owned - 1), index & 3
    bp, bz, bk = parts_of(iota((R, M), 1))
    ap, az, ak = parts_of(iota((M, R), 0))
    wanted = picks(ap, ak, R) == iota((M, R), 1)
    source = (4 * bp + bk) == iota((R, M), 0)
    big_h = jnp.zeros((M, M), F32)
    big_l = jnp.zeros((M, M), F32)
    for zz in range(owned):
        left = jnp.where(wanted & (az == zz), 1.0, 0.0).astype(BF16)
        right = jnp.where(source & (bz == zz), 1.0, 0.0).astype(BF16)
        rh, rl = split(rx[zz])
        for part, add in ((rh, 0), (rl, 1)):
            chosen = jnp.dot(left, part, preferred_element_type=F32).astype(BF16)
            moved = jnp.dot(chosen, right, preferred_element_type=F32)
            if add == 0:
                big_h = big_h + moved
            else:
                big_l = big_l + moved
    recm[:, 0:M] = big_h.astype(BF16)
    recm[:, M:2 * M] = big_h.astype(BF16)
    recm[:, 2 * M:3 * M] = big_l.astype(BF16)

    for k in (3, 5, 6, 7):
        loads[k].wait()

    def prep_y(z, carry):
        h, l = split(by[z])
        byc[z, :, 0:Y] = h
        byc[z, :, Y:2 * Y] = h
        byc[z, :, 2 * Y:3 * Y] = l
        return carry

    lax.fori_loop(0, NZ, prep_y, 0, unroll=4)

    flat = jnp.concatenate([sx[z] for z in range(NZ)], axis=0)
    sxp[...] = jnp.transpose(flat, (1, 0))

    spread_z = iota((NZ, Y), 0)
    spread_l = iota((NZ, Y), 1)
    coeff = jnp.zeros((4 * m, Y), F32)
    for jj in range(4):
        off = jj - 2 if jj < 2 else jj + 2
        pick = lax.rem(4 * j + off + 4 * m, 4 * m)
        spread = jnp.where(spread_l == 4 * spread_z + jj, 1.0, 0.0)
        coeff = coeff + jnp.dot(ry[pick], spread, precision=HIGH, preferred_element_type=F32)
    ryc[...] = coeff

    for t in range(n - 1):
        rim_copy(t).wait_recv()
    vh, vl = split(rrecv[...].reshape(M, Y))
    w = jnp.dot(recm[...], jnp.concatenate([vh, vl, vh], axis=0), preferred_element_type=F32)
    wsend[...] = w.reshape(n, 4 * owned, Y)

    def w_copy(t):
        who = lax.rem(i + 1 + t, n)
        return remote(wsend.at[who], wrecv.at[i], w_s.at[t], w_r.at[t], (who, j))

    for t in range(n - 1):
        w_copy(t).start()
    wrecv[i] = wsend[i]

    def plane_y(q, zz, packed):
        z = q * owned + zz
        w = wrecv[q]
        spikes = pltpu.roll(sxp[...], lax.rem(Y - 4 * z, Y), 1)
        xsol = xl[z]
        for k in range(4):
            xsol = xsol - spikes[:, k:k + 1] * w[4 * zz + k:4 * zz + k + 1, :]
        xh, xlow = split(xsol)
        lin = lax.dot_general(
            jnp.concatenate([xh, xlow, xh], axis=1), byc[z],
            (((1,), (1,)), ((), ())), preferred_element_type=F32)
        yfull[z] = lin
        return jnp.where(group == z, pltpu.roll(lin, lax.rem(4 * z + 2, Y), 1), packed)

    packed = jnp.zeros((X, Y), F32)
    for zz in range(owned):
        packed = plane_y(i, zz, packed)

    def step_y(t, packed):
        w_copy(t).wait_recv()
        who = lax.rem(i + n - 1 - t, n)
        for zz in range(owned):
            packed = plane_y(who, zz, packed)
        return packed

    packed = lax.fori_loop(0, n - 1, step_y, packed)
    yrims[j] = jnp.where(low, pltpu.roll(packed, Y - 2, 1), pltpu.roll(packed, 2, 1))

    def g_copy(t):
        who = lax.rem(j + 1 + t, m)
        return remote(yrims.at[j], yrims.at[j], g_s.at[t], g_r.at[t], (i, who))

    for t in range(m - 1):
        g_copy(t).start()
    for t in range(m - 1):
        g_copy(t).wait_recv()

    total = jnp.zeros((X, Y), F32)
    klane = iota((1, Y), 1) & 3
    for g in range(m):
        field = yrims[g]
        for d in range(-3, 4):
            factor = jnp.zeros((1, Y), F32)
            for jj in range(4):
                if 0 <= jj - d < 4:
                    factor = jnp.where(klane == jj, ryc[4 * g + jj - d:4 * g + jj - d + 1, :], factor)
            total = total + factor * (field if d == 0 else pltpu.roll(field, d % Y, 1))
    cs[...] = total

    def finish(z, carry):
        mine = pltpu.roll(cs[...], lax.rem(Y - 4 * z, Y), 1)
        spikes = sy[z]
        value = yfull[z]
        for k in range(4):
            value = value - mine[:, k:k + 1] * spikes[k:k + 1, :]
        out[z] = value
        return carry

    chunks = 4
    size = NZ // chunks
    stores = []
    for k in range(chunks):
        lax.fori_loop(k * size, (k + 1) * size, finish, 0, unroll=2)
        store = pltpu.make_async_copy(
            out.at[pl.ds(k * size, size)], out_h.at[pl.ds(k * size, size)], out_sem.at[k])
        store.start()
        stores.append(store)
    for copy in halo:
        copy.wait_send()
    for t in range(n - 1):
        rim_copy(t).wait_send()
        w_copy(t).wait_send()
    for t in range(m - 1):
        g_copy(t).wait_send()
    for store in stores:
        store.wait()


def body(conc, mobility, block_x, spike_x, reduced_x, block_y, spike_y, reduced_y):
    n, m = lax.axis_size("gx"), lax.axis_size("gy")
    NZ, X, Y = conc.shape
    owned = NZ // n
    M = 4 * NZ
    nside = 1 if m == 2 else 2
    vm = lambda *shape: pltpu.VMEM(shape, F32)
    vb = lambda *shape: pltpu.VMEM(shape, BF16)
    dma = lambda *shape: pltpu.SemaphoreType.DMA(shape)
    sxt = jnp.transpose(spike_x, (0, 2, 1))
    syt = jnp.transpose(spike_y, (0, 2, 1))
    ryt = jnp.transpose(reduced_y, (1, 2, 0))
    scratch = [
        vm(NZ, X, Y), vm(NZ, X, Y), vm(NZ, X, X), vm(NZ, 4, X), vm(owned, 4 * n, 4 * n),
        vm(NZ, Y, Y), vm(NZ, 4, Y), vm(4 * m, 4 * m, NZ), vm(NZ, X, Y),
        vm(3, NZ, Y), vm(3, NZ, Y), vm(3, NZ, Y), vm(3, NZ, Y),
        vm(2, X, Y), vm(nside, 2, X, Y), vm(2, nside, 8, Y),
        vm(2, NZ, Y), vm(2, NZ, Y), vm(X, Y), vm(X, Y), vm(X, Y),
        vb(NZ, X, 3 * X), vb(NZ, Y, 3 * Y), vm(NZ, X, Y), vm(NZ, X, Y),
        vm(n, 4 * owned, Y), vm(n, 4 * owned, Y), vb(M, 3 * M),
        vm(n, 4 * owned, Y), vm(n, 4 * owned, Y), vm(X, M), vm(m, X, Y), vm(4 * m, Y),
        dma(8), dma(4), dma(2), dma(2), dma(nside), dma(nside), dma(2, nside), dma(2, nside),
        dma(n - 1), dma(n - 1), dma(n - 1), dma(n - 1), dma(m - 1), dma(m - 1),
    ]
    return pl.pallas_call(
        functools.partial(kernel, n, m),
        out_shape=jax.ShapeDtypeStruct(conc.shape, F32),
        in_specs=[pl.BlockSpec(memory_space=pl.ANY)] * 8,
        out_specs=pl.BlockSpec(memory_space=pl.ANY),
        scratch_shapes=scratch,
        compiler_params=pltpu.CompilerParams(
            collective_id=0, has_side_effects=True, vmem_limit_bytes=40 * 2**20),
        cost_estimate=pl.CostEstimate(flops=10**9, bytes_accessed=8 * 2**20, transcendentals=0),
    )(conc, mobility, block_x, sxt, reduced_x, block_y, syt, ryt)


def solution(mesh):
    in_specs = (
        P(None, "gx", "gy"),
        P(None, "gx", "gy"),
        P(None, "gx", None),
        P(None, "gx", None),
        P(),
        P(None, "gy", None),
        P(None, "gy", None),
        P(),
    )
    out_specs = P(None, "gx", "gy")
    return jax.shard_map(body, mesh=mesh, in_specs=in_specs, out_specs=out_specs, check_vma=False)
```

time: 138 us -> 48.9 us (0.35)
  waiting for transfers between devices: 45.1 us -> 0 us
  Pallas kernels: 0 us -> 38.5 us
  local copies, waits for them, and re-layouts: 30.1 us -> 9.9 us
  matrix products: 17.2 us -> 0 us
  starting transfers between devices: 14.2 us -> 0 us
  between operations: 13.6 us -> 0.02 us
  other arithmetic: 12.6 us -> 0 us
  blocking collectives: 4.94 us -> 0 us
    pallas_call x0 -> x1, Pallas kernels: none -> 38.5 us  [body(): pl.pallas_call(functools.partial(kernel, n, m), out_shape=jax.ShapeDtypeS...]
    all_gather x1 -> x0, waiting for transfers between devices: 35.2 us -> none  [solve_x(): gathered = lax.all_gather(rims, 'gx', axis=1, tiled=True)]
    slice x11 -> x0, local copies, waits for them, and re-layouts: 18.5 us -> none  [the longest x4 6.89 us: extended_2(): last = lax.slice_in_dim(shard, length - width, length, axis=dim)]
    dot_general x6 -> x0, matrix products: 17.2 us -> none  [the longest x1 5.33 us: solve_x(): lin = jnp.einsum('zij,zjn->zin', block_x, field, precision=HIGH)]
    ppermute x8 -> x0, starting transfers between devices: 14.2 us -> none  [the longest x4 12.5 us: extended_2(): after = lax.ppermute(leading, axis, down)]
    ppermute x8 -> x0, waiting for transfers between devices: 9.83 us -> none  [the longest x4 6.5 us: extended_2(): before = lax.ppermute(last, axis, up)]
    unnamed x16 -> x17, local copies, waits for them, and re-layouts: 0.92 us -> 9.9 us
    ppermute x4 -> x0, local copies, waits for them, and re-layouts: 7.59 us -> none  [the longest x2 3.81 us: extended_2(): before = lax.ppermute(last, axis, up)]
  transfers between devices with their start and end apart: 9 -> 0, of which waited for: 7 -> 0; matrix products, arithmetic and copies ran while one was open for 7% -> 0% of each run, Pallas kernels for 0% -> 0%
where the time goes in v1:
time: 48.9 us; the launch traced here: 48.4 us
  Pallas kernels  38.5 us (79%)
  local copies, waits for them, and re-layouts  9.9 us (20%)
    pallas_call x1, Pallas kernels, body(): pl.pallas_call(functools.partial(kernel, n, m), out_shape=jax.ShapeDtypeS...  38.5 us
    unnamed x17, local copies, waits for them, and re-layouts  9.9 us

profile of v1, /device:TPU:0, one launch (start us, length us, event | category | flops | bytes accessed | tf_op | source)
XLA Modules:
  0.0 48.4 jit_solution(17931316764399105919)
XLA Ops:
  0.0 0.0 copy-start
  0.0 1.6 %copy-done = f32[32,128,128]{2,1,0:T(8,128)S(1)} copy-done((f32[32,128,128]{2,1,0:T(8,128)S(1)}, f32[32,128,128]{2,1,0:T(8,128)}, u32[]{:S(2)}) %copy-start) | copy-done | bytes 2097176
  1.6 0.0 copy-start.1
  1.6 1.2 %copy-done.1 = f32[32,64,128]{2,1,0:T(8,128)S(1)} copy-done((f32[32,64,128]{2,1,0:T(8,128)S(1)}, f32[32,64,128]{2,1,0:T(8,128)}, u32[]{:S(2)}) %copy-start.1) | copy-done | bytes 1048600
  2.8 0.0 copy-start.2
  2.8 1.2 %copy-done.2 = f32[32,64,128]{2,1,0:T(8,128)S(1)} copy-done((f32[32,64,128]{2,1,0:T(8,128)S(1)}, f32[32,64,128]{2,1,0:T(8,128)}, u32[]{:S(2)}) %copy-start.2) | copy-done | bytes 1048600
  4.0 0.0 copy-start.3
  4.0 1.2 %copy-done.3 = f32[32,64,64]{2,1,0:T(8,128)S(1)} copy-done((f32[32,64,64]{2,1,0:T(8,128)S(1)}, f32[32,64,64]{2,1,0:T(8,128)}, u32[]{:S(2)}) %copy-start.3) | copy-done | bytes 524312
  5.3 0.0 copy-start.4
  5.3 1.2 %copy-done.4 = f32[32,64,64]{2,1,0:T(8,128)S(1)} copy-done((f32[32,64,64]{2,1,0:T(8,128)S(1)}, f32[32,64,64]{2,1,0:T(8,128)}, u32[]{:S(2)}) %copy-start.4) | copy-done | bytes 524312
  6.5 0.0 copy-start.5
  6.5 0.8 %copy-done.5 = f32[32,64,4]{1,2,0:T(4,128)S(1)} copy-done((f32[32,64,4]{1,2,0:T(4,128)S(1)}, f32[32,64,4]{1,2,0:T(4,128)}, u32[]{:S(2)}) %copy-start.5) | copy-done | bytes 32792
  7.3 0.0 copy-start.6
  7.3 0.8 %copy-done.6 = f32[32,128,4]{1,2,0:T(4,128)S(1)} copy-done((f32[32,128,4]{1,2,0:T(4,128)S(1)}, f32[32,128,4]{1,2,0:T(4,128)}, u32[]{:S(2)}) %copy-start.6) | copy-done | bytes 65560
  8.2 0.0 copy-start.7
  8.2 0.8 %copy-done.7 = f32[32,8,8]{0,2,1:T(8,128)S(1)} copy-done((f32[32,8,8]{0,2,1:T(8,128)S(1)}, f32[32,8,8]{0,2,1:T(8,128)}, u32[]{:S(2)}) %copy-start.7) | copy-done | bytes 8216
  8.9 38.5 %shard_map.82 = f32[32,64,128]{2,1,0:T(8,128)S(1)} custom-call(f32[32,64,128]{2,1,0:T(8,128)S(1)} %copy-done.1, f32[32,64,128]{2,1,0:T(8,128)S(1)} %copy-done.2, f32[32,64,64]{2,1,0:T(8,128)S(1)} %copy-done.3, f32[32,4,64]{2,1,0:T(4,128)S(1)} %bitcast.3, f32[32,64,64]{2,1,0:T(8,128)S(1)} %copy-done.4, f32[32,128,128]{2,1,0:T(8,128)S(1)} %copy-done, ...), custom_call_target="tpu_custom_call" | custom-call | flops 1000000000 | bytes 8388608 | tf_op jit(solution)/shard_map/pallas_call | solution.py:369
  47.5 1.0 %copy.10 = f32[32,64,128]{2,1,0:T(8,128)} copy(f32[32,64,128]{2,1,0:T(8,128)S(1)} %shard_map.82) | data formatting | bytes 2097152
Async XLA Ops:
  0.0 1.6 %copy-start = (f32[32,128,128]{2,1,0:T(8,128)S(1)}, f32[32,128,128]{2,1,0:T(8,128)}, u32[]{:S(2)}) copy-start(f32[32,128,128]{2,1,0:T(8,128)} %by_h.1) | copy-start | bytes 6291460
  1.6 1.2 %copy-start.1 = (f32[32,64,128]{2,1,0:T(8,128)S(1)}, f32[32,64,128]{2,1,0:T(8,128)}, u32[]{:S(2)}) copy-start(f32[32,64,128]{2,1,0:T(8,128)} %conc_h.1) | copy-start | bytes 3145732
  2.8 1.2 %copy-start.2 = (f32[32,64,128]{2,1,0:T(8,128)S(1)}, f32[32,64,128]{2,1,0:T(8,128)}, u32[]{:S(2)}) copy-start(f32[32,64,128]{2,1,0:T(8,128)} %mob_h.1) | copy-start | bytes 3145732
  4.0 1.2 %copy-start.3 = (f32[32,64,64]{2,1,0:T(8,128)S(1)}, f32[32,64,64]{2,1,0:T(8,128)}, u32[]{:S(2)}) copy-start(f32[32,64,64]{2,1,0:T(8,128)} %bx_h.1) | copy-start | bytes 1572868
  5.3 1.2 %copy-start.4 = (f32[32,64,64]{2,1,0:T(8,128)S(1)}, f32[32,64,64]{2,1,0:T(8,128)}, u32[]{:S(2)}) copy-start(f32[32,64,64]{2,1,0:T(8,128)} %rx_h.1) | copy-start | bytes 1572868
  6.5 0.8 %copy-start.5 = (f32[32,64,4]{1,2,0:T(4,128)S(1)}, f32[32,64,4]{1,2,0:T(4,128)}, u32[]{:S(2)}) copy-start(f32[32,64,4]{1,2,0:T(4,128)} %param.11) | copy-start | bytes 98308
  7.3 0.8 %copy-start.6 = (f32[32,128,4]{1,2,0:T(4,128)S(1)}, f32[32,128,4]{1,2,0:T(4,128)}, u32[]{:S(2)}) copy-start(f32[32,128,4]{1,2,0:T(4,128)} %param.14) | copy-start | bytes 196612
  8.2 0.8 %copy-start.7 = (f32[32,8,8]{0,2,1:T(8,128)S(1)}, f32[32,8,8]{0,2,1:T(8,128)}, u32[]{:S(2)}) copy-start(f32[32,8,8]{0,2,1:T(8,128)} %param.15) | copy-start | bytes 24580

commit v2 on v1

--- a/solution.py
+++ b/solution.py
@@ -40,6 +40,7 @@
     xs_dn, xs_up, xr_dn, xr_up, ys, yr, cr,
     mux, mobx, mus, mobs, cs,
     bxc, byc, xl, yfull, rims, rrecv, recm, wsend, wrecv, sxp, yrims, ryc,
+    mu_ref, sumx, sumy, sxb,
     load_sem, out_sem, xsem_s, xsem_r, ysem_s, ysem_r, csem_s, csem_r,
     a_s, a_r, w_s, w_r, g_s, g_r,
 ):
@@ -120,8 +121,28 @@
 
     lax.fori_loop(0, NZ, prep_x, 0, unroll=4)
 
+    fwd = lambda a: pltpu.roll(a, 1, 1)
+    bwd = lambda a: pltpu.roll(a, Y - 1, 1)
+
+    def prep_mu(z, carry):
+        c = c_ref[z]
+        around = (jnp.where(lane == 0, 0.0, fwd(c)) + jnp.where(lane == Y - 1, 0.0, bwd(c))
+                  + jnp.where(row == 0, 0.0, pltpu.roll(c, 1, 0))
+                  + jnp.where(row == X - 1, 0.0, pltpu.roll(c, X - 1, 0)))
+        mu_ref[z] = c * c * c - c - (around - 4.0 * c)
+        mob = mobile(b_ref[z], c)
+        b_ref[z] = mob
+        sumx[z] = mob + pltpu.roll(mob, X - 1, 0)
+        sumy[z] = mob + bwd(mob)
+        return carry
+
+    lax.fori_loop(0, NZ, prep_mu, 0, unroll=4)
+
     for copy in halo:
         copy.wait_recv()
+
+    mu_ref[:, 0, :] = mu_ref[:, 0, :] - xr_dn[1]
+    mu_ref[:, X - 1, :] = mu_ref[:, X - 1, :] - xr_up[0]
 
     lo_slot, hi_slot = (0, 0) if m == 2 else (0, 1)
     k4 = lane & 3
@@ -132,8 +153,6 @@
     low1 = low[0:1]
     cd = jnp.where(low1, cr[0, lo_slot, 7:8, :], cr[0, hi_slot, 7:8, :])
     cu = jnp.where(low1, cr[1, lo_slot, 0:1, :], cr[1, hi_slot, 0:1, :])
-    fwd = lambda a: pltpu.roll(a, 1, 1)
-    bwd = lambda a: pltpu.roll(a, Y - 1, 1)
     sum_y = jnp.where(low, fwd(ec) + bwd(pc), bwd(ec) + fwd(pc))
     sum_x = (jnp.where(row == 0, cd, pltpu.roll(ec, 1, 0))
              + jnp.where(row == X - 1, cu, pltpu.roll(ec, X - 1, 0)))
@@ -157,27 +176,24 @@
         mux[s] = near * near * near - near - (far + own + side_lo + side_hi - 4.0 * near)
         mobx[s] = mobile((xr_dn if s == 0 else xr_up)[2], near)
 
+    edge_y = (lane == 0) | (lane == Y - 1)
+    first_y, last_y, first_x, last_x = lane == 0, lane == Y - 1, row == 0, row == X - 1
+
     def plane_x(q, zz):
         z = q * owned + zz
-        c = c_ref[z]
         unpack = Y - 2 - 4 * z
-        cy = pltpu.roll(cs[...], unpack, 1)
-        c_ym = jnp.where(lane == 0, cy, fwd(c))
-        c_yp = jnp.where(lane == Y - 1, cy, bwd(c))
-        c_xm = jnp.where(row == 0, xr_dn[1, pl.ds(z, 1), :], pltpu.roll(c, 1, 0))
-        c_xp = jnp.where(row == X - 1, xr_up[0, pl.ds(z, 1), :], pltpu.roll(c, X - 1, 0))
-        mu = c * c * c - c - (c_xm + c_xp + c_ym + c_yp - 4.0 * c)
-        mob = mobile(b_ref[z], c)
+        mob = b_ref[z]
+        mu = mu_ref[z] - jnp.where(edge_y, pltpu.roll(cs[...], unpack, 1), 0.0)
         muy = pltpu.roll(mus[...], unpack, 1)
-        moby = pltpu.roll(mobs[...], unpack, 1)
-        fy = (jnp.where(lane == Y - 1, moby, bwd(mob)) + mob) * (jnp.where(lane == Y - 1, muy, bwd(mu)) - mu)
-        fy_m = jnp.where(lane == 0, (mob + moby) * (mu - muy), fwd(fy))
+        moby = mob + pltpu.roll(mobs[...], unpack, 1)
+        fy = jnp.where(last_y, moby, sumy[z]) * (jnp.where(last_y, muy, bwd(mu)) - mu)
+        fy_m = jnp.where(first_y, moby * (mu - muy), fwd(fy))
         mu_dn, mu_up = mux[0, pl.ds(z, 1), :], mux[1, pl.ds(z, 1), :]
         mob_dn, mob_up = mobx[0, pl.ds(z, 1), :], mobx[1, pl.ds(z, 1), :]
-        fx = ((jnp.where(row == X - 1, mob_up, pltpu.roll(mob, X - 1, 0)) + mob)
-              * (jnp.where(row == X - 1, mu_up, pltpu.roll(mu, X - 1, 0)) - mu))
-        fx_m = jnp.where(row == 0, (mob + mob_dn) * (mu - mu_dn), pltpu.roll(fx, 1, 0))
-        rhs = c + 0.01 * ((fy - fy_m) + (fx - fx_m))
+        fx = (jnp.where(last_x, mob_up + mob, sumx[z])
+              * (jnp.where(last_x, mu_up, pltpu.roll(mu, X - 1, 0)) - mu))
+        fx_m = jnp.where(first_x, (mob + mob_dn) * (mu - mu_dn), pltpu.roll(fx, 1, 0))
+        rhs = c_ref[z] + 0.01 * ((fy - fy_m) + (fx - fx_m))
         rh, rl = split(rhs)
         lin = jnp.dot(bxc[z], jnp.concatenate([rh, rl, rh], axis=0), preferred_element_type=F32)
         xl[z] = lin
@@ -188,16 +204,22 @@
         who = lax.rem(i + 1 + t, n)
         return remote(rims.at[who], rrecv.at[i], a_s.at[t], a_r.at[t], (who, j))
 
-    def step_x(t, carry):
-        who = lax.rem(i + 1 + t, n)
-        for zz in range(owned):
-            plane_x(who, zz)
-        rim_copy(t).start()
-        return carry
-
-    lax.fori_loop(0, n - 1, step_x, 0)
-    for zz in range(owned):
-        plane_x(i, zz)
+    owners = max(1, 8 // owned)
+
+    def step_x(b, carry):
+        for u in range(owners):
+            who = lax.rem(i + 1 + b * owners + u, n)
+            for zz in range(owned):
+                plane_x(who, zz)
+        for u in range(owners):
+            t = b * owners + u
+
+            @pl.when(t < n - 1)
+            def _():
+                rim_copy(t).start()
+        return carry
+
+    lax.fori_loop(0, n // owners, step_x, 0)
     rrecv[i] = rims[i]
 
     loads[4].wait()
@@ -225,20 +247,19 @@
     recm[:, M:2 * M] = big_h.astype(BF16)
     recm[:, 2 * M:3 * M] = big_l.astype(BF16)
 
-    for k in (3, 5, 6, 7):
+    for k in (3, 7):
         loads[k].wait()
-
-    def prep_y(z, carry):
-        h, l = split(by[z])
-        byc[z, :, 0:Y] = h
-        byc[z, :, Y:2 * Y] = h
-        byc[z, :, 2 * Y:3 * Y] = l
-        return carry
-
-    lax.fori_loop(0, NZ, prep_y, 0, unroll=4)
 
     flat = jnp.concatenate([sx[z] for z in range(NZ)], axis=0)
     sxp[...] = jnp.transpose(flat, (1, 0))
+
+    def prep_spikes(z, carry):
+        spikes = pltpu.roll(sxp[...], lax.rem(Y - 4 * z, Y), 1)
+        for k in range(4):
+            sxb[z, k] = jnp.broadcast_to(spikes[:, k:k + 1], (X, Y))
+        return carry
+
+    lax.fori_loop(0, NZ, prep_spikes, 0, unroll=4)
 
     spread_z = iota((NZ, Y), 0)
     spread_l = iota((NZ, Y), 1)
@@ -264,13 +285,24 @@
         w_copy(t).start()
     wrecv[i] = wsend[i]
 
+    for k in (5, 6):
+        loads[k].wait()
+
+    def prep_y(z, carry):
+        h, l = split(by[z])
+        byc[z, :, 0:Y] = h
+        byc[z, :, Y:2 * Y] = h
+        byc[z, :, 2 * Y:3 * Y] = l
+        return carry
+
+    lax.fori_loop(0, NZ, prep_y, 0, unroll=4)
+
     def plane_y(q, zz, packed):
         z = q * owned + zz
         w = wrecv[q]
-        spikes = pltpu.roll(sxp[...], lax.rem(Y - 4 * z, Y), 1)
         xsol = xl[z]
         for k in range(4):
-            xsol = xsol - spikes[:, k:k + 1] * w[4 * zz + k:4 * zz + k + 1, :]
+            xsol = xsol - sxb[z, k] * w[4 * zz + k:4 * zz + k + 1, :]
         xh, xlow = split(xsol)
         lin = lax.dot_general(
             jnp.concatenate([xh, xlow, xh], axis=1), byc[z],
@@ -278,18 +310,20 @@
         yfull[z] = lin
         return jnp.where(group == z, pltpu.roll(lin, lax.rem(4 * z + 2, Y), 1), packed)
 
-    packed = jnp.zeros((X, Y), F32)
-    for zz in range(owned):
-        packed = plane_y(i, zz, packed)
-
-    def step_y(t, packed):
-        w_copy(t).wait_recv()
-        who = lax.rem(i + n - 1 - t, n)
-        for zz in range(owned):
-            packed = plane_y(who, zz, packed)
+    def step_y(b, packed):
+        for u in range(owners):
+            t = b * owners + u
+
+            @pl.when(t < n - 1)
+            def _():
+                w_copy(t).wait_recv()
+        for u in range(owners):
+            who = lax.rem(i + 2 * n - 1 - b * owners - u, n)
+            for zz in range(owned):
+                packed = plane_y(who, zz, packed)
         return packed
 
-    packed = lax.fori_loop(0, n - 1, step_y, packed)
+    packed = lax.fori_loop(0, n // owners, step_y, jnp.zeros((X, Y), F32))
     yrims[j] = jnp.where(low, pltpu.roll(packed, Y - 2, 1), pltpu.roll(packed, 2, 1))
 
     def g_copy(t):
@@ -326,7 +360,7 @@
     size = NZ // chunks
     stores = []
     for k in range(chunks):
-        lax.fori_loop(k * size, (k + 1) * size, finish, 0, unroll=2)
+        lax.fori_loop(k * size, (k + 1) * size, finish, 0, unroll=8)
         store = pltpu.make_async_copy(
             out.at[pl.ds(k * size, size)], out_h.at[pl.ds(k * size, size)], out_sem.at[k])
         store.start()
@@ -363,6 +397,7 @@
         vb(NZ, X, 3 * X), vb(NZ, Y, 3 * Y), vm(NZ, X, Y), vm(NZ, X, Y),
         vm(n, 4 * owned, Y), vm(n, 4 * owned, Y), vb(M, 3 * M),
         vm(n, 4 * owned, Y), vm(n, 4 * owned, Y), vm(X, M), vm(m, X, Y), vm(4 * m, Y),
+        vm(NZ, X, Y), vm(NZ, X, Y), vm(NZ, X, Y), vm(NZ, 4, X, Y),
         dma(8), dma(4), dma(2), dma(2), dma(nside), dma(nside), dma(2, nside), dma(2, nside),
         dma(n - 1), dma(n - 1), dma(n - 1), dma(n - 1), dma(m - 1), dma(m - 1),
     ]
@@ -373,7 +408,7 @@
         out_specs=pl.BlockSpec(memory_space=pl.ANY),
         scratch_shapes=scratch,
         compiler_params=pltpu.CompilerParams(
-            collective_id=0, has_side_effects=True, vmem_limit_bytes=40 * 2**20),
+            collective_id=0, has_side_effects=True, vmem_limit_bytes=60 * 2**20),
         cost_estimate=pl.CostEstimate(flops=10**9, bytes_accessed=8 * 2**20, transcendentals=0),
     )(conc, mobility, block_x, sxt, reduced_x, block_y, syt, ryt)
 

time: 48.9 us -> 35.9 us (0.73)
  local copies, waits for them, and re-layouts: 9.9 us -> 2.31 us
  Pallas kernels: 38.5 us -> 33.4 us
    unnamed x17 -> x1, local copies, waits for them, and re-layouts: 9.9 us -> 2.31 us
    pallas_call x1, Pallas kernels: 38.5 us -> 33.4 us  [body(): pl.pallas_call(functools.partial(kernel, n, m), out_shape=jax.ShapeDtypeS...]
where the time goes in v2:
time: 35.9 us; the launch traced here: 35.8 us
  Pallas kernels  33.4 us (93%)
  local copies, waits for them, and re-layouts  2.31 us (6%)
    pallas_call x1, Pallas kernels, body(): pl.pallas_call(functools.partial(kernel, n, m), out_shape=jax.ShapeDtypeS...  33.4 us
    unnamed x1, local copies, waits for them, and re-layouts  2.31 us

profile of v2, /device:TPU:0, one launch (start us, length us, event | category | flops | bytes accessed | tf_op | source)
XLA Modules:
  0.0 35.8 jit_solution(5832670137295852674)
XLA Ops:
  0.0 33.4 %shard_map.82 = f32[32,64,128]{2,1,0:T(8,128)} custom-call(f32[32,64,128]{2,1,0:T(8,128)} %conc_h.1, f32[32,64,128]{2,1,0:T(8,128)} %mob_h.1, f32[32,64,64]{2,1,0:T(8,128)} %bx_h.1, f32[32,4,64]{2,1,0:T(4,128)} %bitcast.3, f32[32,64,64]{2,1,0:T(8,128)} %rx_h.1, f32[32,128,128]{2,1,0:T(8,128)} %by_h.1, f32[32,4,128]{2,1,0:T(4,128)} %bitcast.4, ...), custom_call_target="tpu_custom_call" | custom-call | flops 1000000000 | bytes 8388608 | tf_op jit(solution)/shard_map/pallas_call | solution.py:404
  33.4 2.3 %copy.10 = f32[32,64,128]{2,1,0:T(8,128)} copy(f32[32,64,128]{2,1,0:T(8,128)} %shard_map.82) | data formatting | bytes 2097152

commit v3 on v2

--- a/solution.py
+++ b/solution.py
@@ -35,11 +35,11 @@
 
 def kernel(
     n, m,
-    conc_h, mob_h, bx_h, sx_h, rx_h, by_h, sy_h, ry_h, out_h,
-    c_ref, b_ref, bx, sx, rx, by, sy, ry, out,
+    conc_h, mob_h, bx_h, sx_h, rx_h, by_h, ry_h, lin_h, total_h,
+    c_ref, b_ref, bx, sx, rx, by, ry,
     xs_dn, xs_up, xr_dn, xr_up, ys, yr, cr,
     mux, mobx, mus, mobs, cs,
-    bxc, byc, xl, yfull, rims, rrecv, recm, wsend, wrecv, sxp, yrims, ryc,
+    bxc, byc, xl, yfull, rims, rrecv, recm, wsend, wrecv, sxp, yrims, ryc, byr, byr3, sx3, total_v,
     mu_ref, sumx, sumy, sxb,
     load_sem, out_sem, xsem_s, xsem_r, ysem_s, ysem_r, csem_s, csem_r,
     a_s, a_r, w_s, w_r, g_s, g_r,
@@ -58,11 +58,11 @@
         pltpu.make_async_copy(src, dst, load_sem.at[k])
         for k, (src, dst) in enumerate((
             (conc_h, c_ref), (mob_h, b_ref), (bx_h, bx), (sx_h, sx),
-            (rx_h.at[pl.ds(i * owned, owned)], rx), (by_h, by), (sy_h, sy), (ry_h, ry),
+            (rx_h.at[pl.ds(i * owned, owned)], rx), (by_h, by), (ry_h, ry),
         ))
     ]
-    for load in loads:
-        load.start()
+    loads[0].start()
+    loads[1].start()
 
     barrier = pltpu.get_barrier_semaphore()
     peers = [(lax.rem(i + t, n), j) for t in range(1, n)]
@@ -73,6 +73,8 @@
 
     loads[0].wait()
     loads[1].wait()
+    for load in loads[2:]:
+        load.start()
     xs_dn[0] = c_ref[:, 0, :]
     xs_dn[1] = c_ref[:, 1, :]
     xs_dn[2] = b_ref[:, 0, :]
@@ -88,8 +90,13 @@
         mine = group == z
         pc = jnp.where(mine, pltpu.roll(c_ref[z], (4 * z + 2) % Y, 1), pc)
         pb = jnp.where(mine, pltpu.roll(b_ref[z], (4 * z + 2) % Y, 1), pb)
-    ys[0] = pc
-    ys[1] = pb
+    fwd = lambda a: pltpu.roll(a, 1, 1)
+    bwd = lambda a: pltpu.roll(a, Y - 1, 1)
+    half = X // 2
+    kh = iota((half, Y), 1) & 3
+    ys[0:X] = pc
+    ys[X:X + half] = jnp.where(
+        kh == 0, bwd(pb[half:X]), jnp.where(kh == 3, fwd(pb[half:X]), pb[0:half]))
 
     pl.semaphore_wait(barrier, len(peers))
 
@@ -105,8 +112,8 @@
     for k, side in enumerate(sides):
         slot = k if m == 2 else 1 - k
         halo.append(remote(ys, yr.at[slot], ysem_s.at[k], ysem_r.at[k], (i, side)))
-        halo.append(remote(ys.at[0, 0:8], cr.at[1, slot], csem_s.at[0, k], csem_r.at[0, k], (dn, side)))
-        halo.append(remote(ys.at[0, X - 8:X], cr.at[0, slot], csem_s.at[1, k], csem_r.at[1, k], (up, side)))
+        halo.append(remote(ys.at[0:8], cr.at[1, slot], csem_s.at[0, k], csem_r.at[0, k], (dn, side)))
+        halo.append(remote(ys.at[X - 8:X], cr.at[0, slot], csem_s.at[1, k], csem_r.at[1, k], (up, side)))
     for copy in halo:
         copy.start()
 
@@ -120,9 +127,6 @@
         return carry
 
     lax.fori_loop(0, NZ, prep_x, 0, unroll=4)
-
-    fwd = lambda a: pltpu.roll(a, 1, 1)
-    bwd = lambda a: pltpu.roll(a, Y - 1, 1)
 
     def prep_mu(z, carry):
         c = c_ref[z]
@@ -147,9 +151,12 @@
     lo_slot, hi_slot = (0, 0) if m == 2 else (0, 1)
     k4 = lane & 3
     low = k4 < 2
-    pc = ys[0]
-    ec = jnp.where(low, yr[lo_slot, 0], yr[hi_slot, 0])
-    eb = jnp.where(low, yr[lo_slot, 1], yr[hi_slot, 1])
+    pc = ys[0:X]
+    ec = jnp.where(low, yr[lo_slot, 0:X], yr[hi_slot, 0:X])
+    lo_b, hi_b = yr[lo_slot, X:X + half], yr[hi_slot, X:X + half]
+    eb = jnp.concatenate([
+        jnp.where(kh < 2, lo_b, hi_b),
+        jnp.where(kh < 2, fwd(lo_b), bwd(hi_b))], axis=0)
     low1 = low[0:1]
     cd = jnp.where(low1, cr[0, lo_slot, 7:8, :], cr[0, hi_slot, 7:8, :])
     cu = jnp.where(low1, cr[1, lo_slot, 0:1, :], cr[1, hi_slot, 0:1, :])
@@ -247,11 +254,55 @@
     recm[:, M:2 * M] = big_h.astype(BF16)
     recm[:, 2 * M:3 * M] = big_l.astype(BF16)
 
-    for k in (3, 7):
-        loads[k].wait()
-
+    loads[5].wait()
+
+    def prep_y(z, carry):
+        h, l = split(by[z])
+        byc[z, :, 0:Y] = h
+        byc[z, :, Y:2 * Y] = h
+        byc[z, :, 2 * Y:3 * Y] = l
+        return carry
+
+    lax.fori_loop(0, NZ, prep_y, 0, unroll=4)
+
+    def lin_y(z, packed):
+        xh, xlow = split(xl[z])
+        lin = lax.dot_general(
+            jnp.concatenate([xh, xlow, xh], axis=1), byc[z],
+            (((1,), (1,)), ((), ())), preferred_element_type=F32)
+        yfull[z] = lin
+        return jnp.where(group == z, pltpu.roll(lin, lax.rem(4 * z + 2, Y), 1), packed)
+
+    packed = lax.fori_loop(0, NZ // 2, lin_y, jnp.zeros((X, Y), F32), unroll=8)
+
+    for t in range(n - 1):
+        rim_copy(t).wait_recv()
+    vh, vl = split(rrecv[...].reshape(M, Y))
+    w = jnp.dot(recm[...], jnp.concatenate([vh, vl, vh], axis=0), preferred_element_type=F32)
+    wsend[...] = w.reshape(n, 4 * owned, Y)
+
+    def w_copy(t):
+        who = lax.rem(i + 1 + t, n)
+        return remote(wsend.at[who], wrecv.at[i], w_s.at[t], w_r.at[t], (who, j))
+
+    for t in range(n - 1):
+        w_copy(t).start()
+    wrecv[i] = wsend[i]
+
+    packed = lax.fori_loop(NZ // 2, NZ, lin_y, packed, unroll=8)
+    packed = jnp.where(low, pltpu.roll(packed, Y - 2, 1), pltpu.roll(packed, 2, 1))
+    for z in range(NZ):
+        byr[4 * z:4 * z + 2] = by[z, 0:2, :]
+        byr[4 * z + 2:4 * z + 4] = by[z, Y - 2:Y, :]
+    rh, rl = split(byr[...])
+    byr3[...] = jnp.concatenate([rh, rh, rl], axis=1)
+    loads[3].wait()
+    loads[6].wait()
     flat = jnp.concatenate([sx[z] for z in range(NZ)], axis=0)
-    sxp[...] = jnp.transpose(flat, (1, 0))
+    flat = jnp.transpose(flat, (1, 0))
+    sxp[...] = flat
+    sh, sl = split(flat)
+    sx3[...] = jnp.concatenate([sh, sh, sl], axis=1)
 
     def prep_spikes(z, carry):
         spikes = pltpu.roll(sxp[...], lax.rem(Y - 4 * z, Y), 1)
@@ -272,59 +323,15 @@
     ryc[...] = coeff
 
     for t in range(n - 1):
-        rim_copy(t).wait_recv()
-    vh, vl = split(rrecv[...].reshape(M, Y))
-    w = jnp.dot(recm[...], jnp.concatenate([vh, vl, vh], axis=0), preferred_element_type=F32)
-    wsend[...] = w.reshape(n, 4 * owned, Y)
-
-    def w_copy(t):
-        who = lax.rem(i + 1 + t, n)
-        return remote(wsend.at[who], wrecv.at[i], w_s.at[t], w_r.at[t], (who, j))
-
-    for t in range(n - 1):
-        w_copy(t).start()
-    wrecv[i] = wsend[i]
-
-    for k in (5, 6):
-        loads[k].wait()
-
-    def prep_y(z, carry):
-        h, l = split(by[z])
-        byc[z, :, 0:Y] = h
-        byc[z, :, Y:2 * Y] = h
-        byc[z, :, 2 * Y:3 * Y] = l
-        return carry
-
-    lax.fori_loop(0, NZ, prep_y, 0, unroll=4)
-
-    def plane_y(q, zz, packed):
-        z = q * owned + zz
-        w = wrecv[q]
-        xsol = xl[z]
-        for k in range(4):
-            xsol = xsol - sxb[z, k] * w[4 * zz + k:4 * zz + k + 1, :]
-        xh, xlow = split(xsol)
-        lin = lax.dot_general(
-            jnp.concatenate([xh, xlow, xh], axis=1), byc[z],
-            (((1,), (1,)), ((), ())), preferred_element_type=F32)
-        yfull[z] = lin
-        return jnp.where(group == z, pltpu.roll(lin, lax.rem(4 * z + 2, Y), 1), packed)
-
-    def step_y(b, packed):
-        for u in range(owners):
-            t = b * owners + u
-
-            @pl.when(t < n - 1)
-            def _():
-                w_copy(t).wait_recv()
-        for u in range(owners):
-            who = lax.rem(i + 2 * n - 1 - b * owners - u, n)
-            for zz in range(owned):
-                packed = plane_y(who, zz, packed)
-        return packed
-
-    packed = lax.fori_loop(0, n // owners, step_y, jnp.zeros((X, Y), F32))
-    yrims[j] = jnp.where(low, pltpu.roll(packed, Y - 2, 1), pltpu.roll(packed, 2, 1))
+        w_copy(t).wait_recv()
+    wh, wl = split(wrecv[...].reshape(M, Y))
+    mixed = lax.dot_general(
+        jnp.concatenate([wh, wl, wh], axis=1), byr3[...],
+        (((1,), (1,)), ((), ())), preferred_element_type=F32)
+    mixed = jnp.where((iota((M, M), 0) >> 2) == (iota((M, M), 1) >> 2), mixed, 0.0)
+    mh, ml = split(mixed)
+    yrims[j] = packed - jnp.dot(
+        sx3[...], jnp.concatenate([mh, ml, mh], axis=0), preferred_element_type=F32)
 
     def g_copy(t):
         who = lax.rem(j + 1 + t, m)
@@ -332,6 +339,32 @@
 
     for t in range(m - 1):
         g_copy(t).start()
+
+    def fix_y(b, carry):
+        for u in range(owners):
+            q = b * owners + u
+            fh, fl = split(wrecv[q])
+            for zz in range(owned):
+                z = q * owned + zz
+                part = lax.dot_general(
+                    jnp.concatenate([fh, fl, fh], axis=1), byc[z],
+                    (((1,), (1,)), ((), ())), preferred_element_type=F32)
+                value = yfull[z]
+                for k in range(4):
+                    value = value - sxb[z, k] * part[4 * zz + k:4 * zz + k + 1, :]
+                yfull[z] = value
+        return carry
+
+    groups = n // owners
+    size = NZ // groups
+    stores = []
+    for b in range(groups):
+        fix_y(b, 0)
+        store = pltpu.make_async_copy(
+            yfull.at[pl.ds(b * size, size)], lin_h.at[pl.ds(b * size, size)], out_sem.at[b])
+        store.start()
+        stores.append(store)
+
     for t in range(m - 1):
         g_copy(t).wait_recv()
 
@@ -345,26 +378,10 @@
                 if 0 <= jj - d < 4:
                     factor = jnp.where(klane == jj, ryc[4 * g + jj - d:4 * g + jj - d + 1, :], factor)
             total = total + factor * (field if d == 0 else pltpu.roll(field, d % Y, 1))
-    cs[...] = total
-
-    def finish(z, carry):
-        mine = pltpu.roll(cs[...], lax.rem(Y - 4 * z, Y), 1)
-        spikes = sy[z]
-        value = yfull[z]
-        for k in range(4):
-            value = value - mine[:, k:k + 1] * spikes[k:k + 1, :]
-        out[z] = value
-        return carry
-
-    chunks = 4
-    size = NZ // chunks
-    stores = []
-    for k in range(chunks):
-        lax.fori_loop(k * size, (k + 1) * size, finish, 0, unroll=8)
-        store = pltpu.make_async_copy(
-            out.at[pl.ds(k * size, size)], out_h.at[pl.ds(k * size, size)], out_sem.at[k])
-        store.start()
-        stores.append(store)
+    total_v[...] = total
+    store = pltpu.make_async_copy(total_v, total_h, out_sem.at[groups])
+    store.start()
+    stores.append(store)
     for copy in halo:
         copy.wait_send()
     for t in range(n - 1):
@@ -374,6 +391,17 @@
         g_copy(t).wait_send()
     for store in stores:
         store.wait()
+
+
+def finish(total_ref, spikes_ref, lin_ref, out_ref):
+    size, X, Y = lin_ref.shape
+    base = pl.program_id(0) * size
+    for z in range(size):
+        mine = pltpu.roll(total_ref[...], lax.rem(Y - 4 * (base + z), Y), 1)
+        value = lin_ref[z]
+        for k in range(4):
+            value = value - mine[:, k:k + 1] * spikes_ref[z, k:k + 1, :]
+        out_ref[z] = value
 
 
 def body(conc, mobility, block_x, spike_x, reduced_x, block_y, spike_y, reduced_y):
@@ -390,27 +418,41 @@
     ryt = jnp.transpose(reduced_y, (1, 2, 0))
     scratch = [
         vm(NZ, X, Y), vm(NZ, X, Y), vm(NZ, X, X), vm(NZ, 4, X), vm(owned, 4 * n, 4 * n),
-        vm(NZ, Y, Y), vm(NZ, 4, Y), vm(4 * m, 4 * m, NZ), vm(NZ, X, Y),
+        vm(NZ, Y, Y), vm(4 * m, 4 * m, NZ),
         vm(3, NZ, Y), vm(3, NZ, Y), vm(3, NZ, Y), vm(3, NZ, Y),
-        vm(2, X, Y), vm(nside, 2, X, Y), vm(2, nside, 8, Y),
+        vm(X + X // 2, Y), vm(nside, X + X // 2, Y), vm(2, nside, 8, Y),
         vm(2, NZ, Y), vm(2, NZ, Y), vm(X, Y), vm(X, Y), vm(X, Y),
         vb(NZ, X, 3 * X), vb(NZ, Y, 3 * Y), vm(NZ, X, Y), vm(NZ, X, Y),
         vm(n, 4 * owned, Y), vm(n, 4 * owned, Y), vb(M, 3 * M),
         vm(n, 4 * owned, Y), vm(n, 4 * owned, Y), vm(X, M), vm(m, X, Y), vm(4 * m, Y),
+        vm(M, Y), vb(M, 3 * Y), vb(X, 3 * M), vm(X, Y),
         vm(NZ, X, Y), vm(NZ, X, Y), vm(NZ, X, Y), vm(NZ, 4, X, Y),
-        dma(8), dma(4), dma(2), dma(2), dma(nside), dma(nside), dma(2, nside), dma(2, nside),
+        dma(7), dma(n + 1), dma(2), dma(2), dma(nside), dma(nside), dma(2, nside), dma(2, nside),
         dma(n - 1), dma(n - 1), dma(n - 1), dma(n - 1), dma(m - 1), dma(m - 1),
     ]
-    return pl.pallas_call(
+    lin, total = pl.pallas_call(
         functools.partial(kernel, n, m),
-        out_shape=jax.ShapeDtypeStruct(conc.shape, F32),
-        in_specs=[pl.BlockSpec(memory_space=pl.ANY)] * 8,
-        out_specs=pl.BlockSpec(memory_space=pl.ANY),
+        out_shape=(jax.ShapeDtypeStruct(conc.shape, F32), jax.ShapeDtypeStruct((X, Y), F32)),
+        in_specs=[pl.BlockSpec(memory_space=pl.ANY)] * 7,
+        out_specs=(pl.BlockSpec(memory_space=pl.ANY), pl.BlockSpec(memory_space=pl.ANY)),
         scratch_shapes=scratch,
         compiler_params=pltpu.CompilerParams(
             collective_id=0, has_side_effects=True, vmem_limit_bytes=60 * 2**20),
         cost_estimate=pl.CostEstimate(flops=10**9, bytes_accessed=8 * 2**20, transcendentals=0),
-    )(conc, mobility, block_x, sxt, reduced_x, block_y, syt, ryt)
+    )(conc, mobility, block_x, sxt, reduced_x, block_y, ryt)
+    step = 8
+    return pl.pallas_call(
+        finish,
+        out_shape=jax.ShapeDtypeStruct(conc.shape, F32),
+        grid=(NZ // step,),
+        in_specs=[
+            pl.BlockSpec((X, Y), lambda g: (0, 0)),
+            pl.BlockSpec((step, 4, Y), lambda g: (g, 0, 0)),
+            pl.BlockSpec((step, X, Y), lambda g: (g, 0, 0)),
+        ],
+        out_specs=pl.BlockSpec((step, X, Y), lambda g: (g, 0, 0)),
+        compiler_params=pltpu.CompilerParams(vmem_limit_bytes=60 * 2**20),
+    )(total, syt, lin)
 
 
 def solution(mesh):

time: 35.9 us -> 32.1 us (0.89)
  local copies, waits for them, and re-layouts: 2.31 us -> 0 us
  Pallas kernels: 33.4 us -> 31.8 us
    unnamed x1 -> x0, local copies, waits for them, and re-layouts: 2.31 us -> none
    pallas_call x1 -> x2, Pallas kernels: 33.4 us -> 31.8 us  [the longest x1 26 us: body(): pl.pallas_call(functools.partial(kernel, n, m), out_shape=(jax.ShapeDtype...]
where the time goes in v3:
time: 32.1 us; the launch traced here: 31.8 us
  Pallas kernels  31.8 us (99%)
    pallas_call x1, Pallas kernels, body(): pl.pallas_call(functools.partial(kernel, n, m), out_shape=(jax.ShapeDtype...  26 us
    pallas_call x1, Pallas kernels, body(): pl.pallas_call(finish, out_shape=jax.ShapeDtypeStruct(conc.shape, F32), g...  5.81 us

profile of v3, /device:TPU:0, one launch (start us, length us, event | category | flops | bytes accessed | tf_op | source)
XLA Modules:
  0.0 31.8 jit_solution(8159132799999660406)
XLA Ops:
  0.0 26.0 %shard_map.82 = (f32[32,64,128]{2,1,0:T(8,128)}, f32[64,128]{1,0:T(8,128)}) custom-call(f32[32,64,128]{2,1,0:T(8,128)} %conc_h.1, f32[32,64,128]{2,1,0:T(8,128)} %mob_h.1, f32[32,64,64]{2,1,0:T(8,128)} %bx_h.1, f32[32,4,64]{2,1,0:T(4,128)} %bitcast.3, f32[32,64,64]{2,1,0:T(8,128)} %rx_h.1, f32[32,128,128]{2,1,0:T(8,128)} %by_h.1, f32[8,8,32]{2,1,0:T(8,128)} %bitcast.5), custom_call_target="tpu_custom_call" | custom-call | flops 1000000000 | bytes 8388608 | tf_op jit(solution)/shard_map/pallas_call | solution.py:433
  26.0 5.8 %shard_map.83 = f32[32,64,128]{2,1,0:T(8,128)} custom-call(f32[64,128]{1,0:T(8,128)} %get-tuple-element.7.total_ref, f32[32,4,128]{2,1,0:T(4,128)} %bitcast.4, f32[32,64,128]{2,1,0:T(8,128)} %get-tuple-element.8.lin_ref), custom_call_target="tpu_custom_call" | custom-call | tf_op jit(solution)/shard_map/pallas_call | solution.py:444
